TPU v7x, 32 devices: a whole 2x2x4 slice. The times are simulated.
32 devices in a mesh: items: 8 (over z, x), ffn: 4 (over y, core).
Axes of the slice: x: 2, y: 2, z: 4, core: 2. Of those that a mesh axis runs over, the one named last changes fastest.
Arguments:
- text_rows: bfloat16 [32, 4, 502, 768], P(('items', 'ffn')), may hold values from -6 to 6
- attn_weight: bfloat16 [3072, 768], P(('items', 'ffn'))
- vectors: bfloat16 [18, 768], P(None, ('items', 'ffn'))
- w_in: bfloat16 [768, 3072], P('items', 'ffn'), may hold values from -0.21875 to 0.21875
- b_in: bfloat16 [4, 768], P('ffn', 'items'), may hold values from -1.5 to 1.5
- w_out: bfloat16 [3072, 768], P('ffn', 'items'), may hold values from -0.109375 to 0.109375
- seg_count: int32 [32], P(('items', 'ffn')), may hold values from 2 to 4, as said below
- last_fill: int32 [32], P(('items', 'ffn')), may hold values from 1 to 502, as said below
- out_grad: bfloat16 [32, 4, 502, 768], P(('items', 'ffn')), may hold values from -6 to 6
- mem_grad: float32 [32, 10, 768], P(('items', 'ffn')), may hold values from -6 to 6
Outputs:
- activations: bfloat16 [32, 4, 502, 768], P(('items', 'ffn'))
- final_memory: float32 [32, 10, 768], P(('items', 'ffn'))
- text_grad: float32 [32, 4, 502, 768], P(('items', 'ffn'))
- attn_grad: float32 [3072, 768], P(('items', 'ffn'))
- vector_grad: float32 [18, 768], P(None, ('items', 'ffn'))
- w_in_grad: float32 [768, 3072], P('items', 'ffn')
- b_in_grad: float32 [4, 768], P('ffn', 'items')
- w_out_grad: float32 [3072, 768], P('ffn', 'items')
Inputs may be any that keep to these rules, and one draw needn't show every extreme that they name: `seg_count`: some item has 4 segments. `last_fill`: some item's last segment is full.
All inputs are finite; a program needn't handle non-finite values.
Results may differ from a plain program's by a relative error of at most 0.025.
Values may be sent and summed in bfloat16 or wider, within the bound.
No kernel may reach another device: no remote copies, remote signals or barrier semaphores. Data moves between devices by JAX's collectives and lax.ppermute only.
A program may use at most 384 MiB of HBM per device.

v0:
```python
import jax
import jax.numpy as jnp
from jax import lax
from jax.sharding import PartitionSpec as P

HEADS = 12
HD = 64
MEM = 10
TEXT = 502
SEGS_MAX = 4


epsilon = 1e-12
root_half = 0.7071067811865476
inv_root_tau = 0.3989422804014327


def gelu_value(pre_act):
    return 0.5 * pre_act * (1.0 + lax.erf(pre_act * root_half))


def gelu_slope(pre_act):
    return (
        0.5 * (1.0 + lax.erf(pre_act * root_half))
        + pre_act * jnp.exp(-0.5 * pre_act * pre_act) * inv_root_tau
    )


def norm_forward(value, gain_row, shift_row):
    centered = value - jnp.mean(value, axis=-1, keepdims=True)
    inverse = lax.rsqrt(jnp.mean(centered * centered, axis=-1, keepdims=True) + epsilon)
    normed = centered * inverse
    return (normed * gain_row + shift_row, normed, inverse)


def norm_backward(upstream, normed, inverse, gain_row):
    scaled = upstream * gain_row
    inner_part = (
        scaled
        - jnp.mean(scaled, axis=-1, keepdims=True)
        - normed * jnp.mean(scaled * normed, axis=-1, keepdims=True)
    )
    return (
        inner_part * inverse,
        jnp.sum(upstream * normed, axis=(0, 1)),
        jnp.sum(upstream, axis=(0, 1)),
    )


def body(
    text_rows, attn_weight, vectors, w_in, b_in, w_out, seg_count, last_fill, out_grad, mem_grad
):
    f32 = jnp.float32
    bf16 = jnp.bfloat16
    attn_full, vec_full = (
        lax.all_gather(attn_weight, ("items", "ffn"), axis=0, tiled=True),
        lax.all_gather(vectors, ("items", "ffn"), axis=1, tiled=True),
    )
    in_part, out_part, bias_part = (
        lax.all_gather(w_in, "items", axis=0, tiled=True),
        lax.all_gather(w_out, "items", axis=1, tiled=True),
        lax.all_gather(b_in, "items", axis=1, tiled=True),
    )
    model_width = attn_full.shape[1]
    small_params = vec_full.astype(f32)
    w_three = attn_full[: 3 * model_width].reshape(3, model_width, model_width)
    w_final = attn_full[3 * model_width :]
    bias_three = jnp.stack([small_params[0], jnp.zeros_like(small_params[0]), small_params[1]])[
        :, None, :
    ]
    item_count = text_rows.shape[0]
    seg_rows = TEXT + 2 * MEM
    flat_rows = item_count * seg_rows
    score_scale = HD ** (-0.5)
    w_first, w_second, b_first = (in_part, out_part, bias_part)
    b_first32 = b_first.astype(f32)

    def ffn_forward(h_low):
        source = lax.all_gather(h_low, "ffn", axis=0, tiled=True)
        hidden_pre = jnp.dot(source, w_first, preferred_element_type=f32) + b_first32
        hidden_low = gelu_value(hidden_pre).astype(bf16)
        terms = jnp.dot(hidden_low, w_second, preferred_element_type=f32)
        branch = lax.psum_scatter(
            terms.astype(jnp.bfloat16), "ffn", scatter_dimension=0, tiled=True
        ).astype(jnp.float32)
        return (branch, (source, hidden_pre, hidden_low))

    def segment_forward(memory, part_text, keep_text):
        mem_ones = jnp.ones((item_count, MEM), f32)
        key_keep = jnp.concatenate([mem_ones, keep_text, mem_ones], axis=1)
        joined = jnp.concatenate([memory, part_text.astype(f32), memory], axis=1)
        joined_low = joined.astype(bf16)
        projected = (
            jnp.einsum(
                "nd,cde->cne",
                joined_low.reshape(flat_rows, model_width),
                w_three,
                preferred_element_type=f32,
            )
            + bias_three
        )
        proj_low = projected.astype(bf16).reshape(3, item_count, seg_rows, HEADS, HD)
        queries, key_rows, values = (proj_low[0], proj_low[1], proj_low[2])
        scores = (
            jnp.einsum("iqhd,ikhd->ihqk", queries, key_rows, preferred_element_type=f32)
            * score_scale
        )
        scores = scores + ((key_keep - 1.0) * 1000000000.0)[:, None, None, :]
        row_peak = jnp.max(scores, axis=-1, keepdims=True)
        exponent = jnp.exp(scores - row_peak)
        attn_probs = exponent / jnp.sum(exponent, axis=-1, keepdims=True)
        mixed = jnp.einsum(
            "ihqk,ikhd->iqhd", attn_probs.astype(bf16), values, preferred_element_type=f32
        )
        mixed_low = mixed.astype(bf16).reshape(flat_rows, model_width)
        attn_out = jnp.dot(mixed_low, w_final, preferred_element_type=f32) + small_params[2]
        first_sum = joined + attn_out.reshape(item_count, seg_rows, model_width)
        normed_out, normed_one, inverse_one = norm_forward(
            first_sum, small_params[3], small_params[4]
        )
        h_low = normed_out.astype(bf16).reshape(flat_rows, model_width)
        branch, ffn_state = ffn_forward(h_low)
        second_sum = normed_out + (branch + small_params[5]).reshape(
            item_count, seg_rows, model_width
        )
        result, normed_two, inverse_two = norm_forward(second_sum, small_params[6], small_params[7])
        saved_state = (
            joined_low,
            queries,
            key_rows,
            values,
            attn_probs,
            mixed_low,
            normed_one,
            inverse_one,
            ffn_state,
            normed_two,
            inverse_two,
        )
        return (result, saved_state)

    position = jnp.arange(TEXT, dtype=jnp.int32)

    def text_keep(seg_index):
        active = seg_index < seg_count
        fill_limit = jnp.where(seg_index == seg_count - 1, last_fill, jnp.where(active, TEXT, 0))
        return ((position[None, :] < fill_limit[:, None]).astype(f32), active)

    memory = small_params[8 : 8 + MEM][None]
    stored = []
    outputs = []
    for seg_index in range(SEGS_MAX):
        keep_text, active = text_keep(seg_index)
        stored.append(memory)
        result, saved_state = segment_forward(memory, text_rows[:, seg_index], keep_text)
        outputs.append(result[:, MEM : MEM + TEXT] * keep_text[:, :, None])
        memory = jnp.where(active[:, None, None], result[:, MEM + TEXT :], memory)
    activations = jnp.stack(outputs, axis=1).astype(bf16)
    memory_grad = mem_grad
    text_grads = [None] * SEGS_MAX
    acc_three = jnp.zeros((3, model_width, model_width), f32)
    acc_final = jnp.zeros((model_width, model_width), f32)
    acc_first = jnp.zeros(w_first.shape, f32)
    acc_second = jnp.zeros(w_second.shape, f32)
    acc_bias = jnp.zeros(b_first.shape, f32)
    acc_vec = jnp.zeros((8, model_width), f32)
    for seg_index in reversed(range(SEGS_MAX)):
        keep_text, active = text_keep(seg_index)
        unused, saved_state = segment_forward(stored[seg_index], text_rows[:, seg_index], keep_text)
        (
            joined_low,
            queries,
            key_rows,
            values,
            attn_probs,
            mixed_low,
            normed_one,
            inverse_one,
            ffn_state,
            normed_two,
            inverse_two,
        ) = saved_state
        write_grad = jnp.where(active[:, None, None], memory_grad, 0.0)
        text_part = out_grad[:, seg_index].astype(f32) * keep_text[:, :, None]
        grad_result = jnp.concatenate(
            [jnp.zeros((item_count, MEM, model_width), f32), text_part, write_grad], axis=1
        )
        grad_second_sum, gain_two, shift_two = norm_backward(
            grad_result, normed_two, inverse_two, small_params[6]
        )
        branch_low = grad_second_sum.astype(bf16).reshape(flat_rows, model_width)
        ffn_source, ffn_hidden_pre, ffn_hidden_low = ffn_state
        incoming = lax.all_gather(branch_low, "ffn", axis=0, tiled=True)
        grad_second = jnp.dot(ffn_hidden_low.T, incoming, preferred_element_type=f32)
        grad_hidden = jnp.dot(incoming, w_second.T, preferred_element_type=f32)
        grad_pre = (grad_hidden * gelu_slope(ffn_hidden_pre)).astype(bf16)
        grad_first = jnp.dot(ffn_source.T, grad_pre, preferred_element_type=f32)
        grad_bias = jnp.sum(grad_pre.astype(f32), axis=0, keepdims=True)
        back_terms = jnp.dot(grad_pre, w_first.T, preferred_element_type=f32)
        back_grad = lax.psum_scatter(
            back_terms.astype(jnp.bfloat16), "ffn", scatter_dimension=0, tiled=True
        ).astype(jnp.float32)
        back_grad, grad_first, grad_second, grad_bias = (
            back_grad,
            grad_first,
            grad_second,
            grad_bias,
        )
        grad_normed = grad_second_sum + back_grad.reshape(item_count, seg_rows, model_width)
        grad_first_sum, gain_one, shift_one = norm_backward(
            grad_normed, normed_one, inverse_one, small_params[3]
        )
        attn_low = grad_first_sum.astype(bf16).reshape(flat_rows, model_width)
        grad_final = jnp.dot(mixed_low.T, attn_low, preferred_element_type=f32)
        grad_mixed = jnp.dot(attn_low, w_final.T, preferred_element_type=f32).astype(bf16)
        grad_mixed = grad_mixed.reshape(item_count, seg_rows, HEADS, HD)
        grad_values = jnp.einsum(
            "ihqk,iqhd->ikhd", attn_probs.astype(bf16), grad_mixed, preferred_element_type=f32
        )
        grad_probs = jnp.einsum("iqhd,ikhd->ihqk", grad_mixed, values, preferred_element_type=f32)
        inner_sum = jnp.sum(grad_probs * attn_probs, axis=-1, keepdims=True)
        grad_scores = (attn_probs * (grad_probs - inner_sum)).astype(bf16)
        grad_queries = (
            jnp.einsum("ihqk,ikhd->iqhd", grad_scores, key_rows, preferred_element_type=f32)
            * score_scale
        )
        grad_keys = (
            jnp.einsum("ihqk,iqhd->ikhd", grad_scores, queries, preferred_element_type=f32)
            * score_scale
        )
        grad_proj = (
            jnp.stack([grad_queries, grad_keys, grad_values])
            .astype(bf16)
            .reshape(3, flat_rows, model_width)
        )
        flat_joined = joined_low.reshape(flat_rows, model_width)
        acc_three = acc_three + jnp.einsum(
            "nd,cne->cde", flat_joined, grad_proj, preferred_element_type=f32
        )
        acc_final = acc_final + grad_final
        acc_first = acc_first + grad_first
        acc_second = acc_second + grad_second
        acc_bias = acc_bias + grad_bias
        bias_sums = jnp.sum(grad_proj.astype(f32), axis=1)
        acc_vec = acc_vec + jnp.stack(
            [
                bias_sums[0],
                bias_sums[2],
                jnp.sum(attn_low.astype(f32), axis=0),
                gain_one,
                shift_one,
                jnp.sum(branch_low.astype(f32), axis=0),
                gain_two,
                shift_two,
            ]
        )
        grad_joined = grad_first_sum + jnp.einsum(
            "cne,cde->nd", grad_proj, w_three, preferred_element_type=f32
        ).reshape(item_count, seg_rows, model_width)
        text_grads[seg_index] = grad_joined[:, MEM : MEM + TEXT]
        from_segment = grad_joined[:, :MEM] + grad_joined[:, MEM + TEXT :]
        memory_grad = jnp.where(active[:, None, None], from_segment, memory_grad)
    text_grad = jnp.stack(text_grads, axis=1)
    attn_total = jnp.concatenate(
        [acc_three.reshape(3 * model_width, model_width), acc_final], axis=0
    )
    vec_total = jnp.concatenate([acc_vec, jnp.sum(memory_grad, axis=0)], axis=0)
    attn_grad, vector_grad = (
        lax.psum_scatter(attn_total, ("items", "ffn"), scatter_dimension=0, tiled=True),
        lax.psum_scatter(vec_total, ("items", "ffn"), scatter_dimension=1, tiled=True),
    )
    w_in_grad, w_out_grad, b_in_grad = (
        lax.psum_scatter(
            acc_first.astype(jnp.bfloat16), "items", scatter_dimension=0, tiled=True
        ).astype(jnp.float32),
        lax.psum_scatter(
            acc_second.astype(jnp.bfloat16), "items", scatter_dimension=1, tiled=True
        ).astype(jnp.float32),
        lax.psum_scatter(
            acc_bias.astype(jnp.bfloat16), "items", scatter_dimension=1, tiled=True
        ).astype(jnp.float32),
    )
    return (
        activations,
        memory,
        text_grad,
        attn_grad,
        vector_grad,
        w_in_grad,
        b_in_grad,
        w_out_grad,
    )


def solution(mesh):
    return jax.shard_map(
        body,
        mesh=mesh,
        in_specs=(
            P(("items", "ffn"), None, None, None),
            P(("items", "ffn"), None),
            P(None, ("items", "ffn")),
            P("items", "ffn"),
            P("ffn", "items"),
            P("ffn", "items"),
            P(("items", "ffn")),
            P(("items", "ffn")),
            P(("items", "ffn"), None, None, None),
            P(("items", "ffn"), None, None),
        ),
        out_specs=(
            P(("items", "ffn"), None, None, None),
            P(("items", "ffn"), None, None),
            P(("items", "ffn"), None, None, None),
            P(("items", "ffn"), None),
            P(None, ("items", "ffn")),
            P("items", "ffn"),
            P("ffn", "items"),
            P("ffn", "items"),
        ),
        check_vma=False,
    )
```

profile of v0, /device:TPU:0, one launch (start us, length us, event | category | flops | bytes accessed | tf_op | source)
XLA Modules:
  0.0 1530.0 jit_solution(13342052095501082308)
XLA Ops:
  9.4 44.1 %all_gather.43 = bf16[18,768]{0,1:T(8,128)(2,1)S(1)} all-gather(bf16[18,24]{0,1:T(8,128)(2,1)S(1)} %copy.148), channel_id=1, replica_groups=mesh['items'=8,'ffn'=4] {'items','ffn'}, dimensions={1}, use_global_device_ids=true | all-gather | bytes 28512 | tf_op jit(solution)/shard_map/all_gather | solution.py:57
  55.4 10.4 fusion.232
  66.0 11.4 all-gather.20.cloned.1.call-done
  89.5 9.5 fusion.242
  99.1 7.6 fusion.108
  114.1 20.1 %all-reduce = bf16[768]{0:T(1024)(128)(2,1)S(1)} all-reduce(bf16[768]{0:T(1024)(128)(2,1)S(1)} %dynamic-update-slice), channel_id=1, replica_groups=mesh['items'=8,'ffn'=4] {'items'}, use_global_device_ids=true, to_apply=%add | all-reduce | flops 768 | bytes 3072
  143.6 38.8 %all-gather.22.cloned.1.call-done = bf16[768,768]{1,0:T(8,128)(2,1)} async-done(((bf16[96,768]{1,0:T(8,128)(2,1)}), bf16[768,768]{1,0:T(8,128)(2,1)}) %all-gather.22.cloned.1.call-update) | async-done | bytes 1179664 | tf_op jit(solution)/shard_map/all_gather | solution.py:60
  189.5 34.7 %all-gather.24.cloned.1.call-done = bf16[768,768]{0,1:T(8,128)(2,1)} async-done(((bf16[768,96]{0,1:T(8,128)(2,1)}), bf16[768,768]{0,1:T(8,128)(2,1)}) %all-gather.24.cloned.1.call-update) | async-done | bytes 1179664 | tf_op jit(solution)/shard_map/all_gather | solution.py:61
  230.8 32.8 %fusion = bf16[528,768]{1,0:T(8,128)(2,1)} fusion(bf16[2088,768]{1,0:T(8,128)(2,1)} %convolution_convert_fusion.7), kind=kCustom, calls=%all-reduce-scatter | all-reduce-scatter fusion | flops 1622017 | bytes 4018688
  286.8 9.5 fusion.244
  296.3 7.7 fusion.114
  308.4 10.2 all-gather.30.cloned.1.call-start
  318.6 19.3 %all-gather.28.cloned.1.call-done = bf16[4,522,768]{2,1,0:T(8,128)(2,1)} async-done(((bf16[1,522,768]{2,1,0:T(8,128)(2,1)}), bf16[4,522,768]{2,1,0:T(8,128)(2,1)}) %all-gather.28.cloned.1.call-update) | async-done | bytes 3207184 | tf_op jit(solution)/shard_map/all_gather | solution.py:79
  355.0 32.9 %fusion.1 = bf16[528,768]{1,0:T(8,128)(2,1)} fusion(bf16[2088,768]{1,0:T(8,128)(2,1)} %convolution_convert_fusion.6), kind=kCustom, calls=%all-reduce-scatter.1 | all-reduce-scatter fusion | flops 1622017 | bytes 4018688
  412.3 8.5 fusion.246
  420.8 7.4 fusion.120
  433.0 30.8 %all-gather.30.cloned.1.call-done = bf16[4,522,768]{2,1,0:T(8,128)(2,1)} async-done(((bf16[1,522,768]{2,1,0:T(8,128)(2,1)}), bf16[4,522,768]{2,1,0:T(8,128)(2,1)}) %all-gather.30.cloned.1.call-update) | async-done | bytes 3207184 | tf_op jit(solution)/shard_map/all_gather | solution.py:79
  480.4 32.1 %fusion.2 = bf16[528,768]{1,0:T(8,128)(2,1)S(1)} fusion(bf16[2088,768]{1,0:T(8,128)(2,1)} %convolution_convert_fusion.5), kind=kCustom, calls=%all-reduce-scatter.2 | all-reduce-scatter fusion | flops 1622017 | bytes 4018688
  533.3 9.6 fusion.248
  542.9 7.7 fusion.126
  555.2 10.5 fusion.231
  567.7 20.7 %all-gather.32.cloned.1.call-done = bf16[4,522,768]{2,1,0:T(8,128)(2,1)} async-done(((bf16[1,522,768]{2,1,0:T(8,128)(2,1)}), bf16[4,522,768]{2,1,0:T(8,128)(2,1)}) %all-gather.32.cloned.1.call-update) | async-done | bytes 3207184 | tf_op jit(solution)/shard_map/all_gather | solution.py:79
  605.6 32.9 %fusion.3 = bf16[528,768]{1,0:T(8,128)(2,1)} fusion(bf16[2088,768]{1,0:T(8,128)(2,1)} %convolution_convert_fusion.4), kind=kCustom, calls=%all-reduce-scatter.3 | all-reduce-scatter fusion | flops 1622017 | bytes 4018688
  657.0 33.4 %all-gather.34.cloned.1.call-done = bf16[4,522,768]{2,1,0:T(8,128)(2,1)} async-done(((bf16[1,522,768]{2,1,0:T(8,128)(2,1)}), bf16[4,522,768]{2,1,0:T(8,128)(2,1)}) %all-gather.34.cloned.1.call-update) | async-done | bytes 3207184 | tf_op jit(solution)/shard_map/all_gather | solution.py:193
  694.8 7.7 convert_reduce_fusion.3
  708.3 33.0 %fusion.4 = bf16[528,768]{1,0:T(8,128)(2,1)} fusion(bf16[2088,768]{1,0:T(8,128)(2,1)} %convolution_convert_fusion.3), kind=kCustom, calls=%all-reduce-scatter.4 | all-reduce-scatter fusion | flops 1622017 | bytes 4018688
  761.9 9.8 fusion.129
  771.7 10.3 multiply_reduce_fusion.3
  782.0 11.2 multiply_convert_fusion.3
  815.4 31.2 %all-gather.36.cloned.1.call-done = bf16[4,522,768]{2,1,0:T(8,128)(2,1)} async-done(((bf16[1,522,768]{2,1,0:T(8,128)(2,1)}), bf16[4,522,768]{2,1,0:T(8,128)(2,1)}) %all-gather.36.cloned.1.call-update) | async-done | bytes 3207184 | tf_op jit(solution)/shard_map/all_gather | solution.py:193
  851.0 7.7 convert_reduce_fusion.2
  864.7 33.0 %fusion.5 = bf16[528,768]{1,0:T(8,128)(2,1)} fusion(bf16[2088,768]{1,0:T(8,128)(2,1)} %convolution_convert_fusion.2), kind=kCustom, calls=%all-reduce-scatter.5 | all-reduce-scatter fusion | flops 1622017 | bytes 4018688
  916.9 9.5 fusion.123
  926.4 15.0 multiply_reduce_fusion.2
  980.6 22.2 %all-gather.38.cloned.1.call-done = bf16[4,522,768]{2,1,0:T(8,128)(2,1)} async-done(((bf16[1,522,768]{2,1,0:T(8,128)(2,1)}), bf16[4,522,768]{2,1,0:T(8,128)(2,1)}) %all-gather.38.cloned.1.call-update) | async-done | bytes 3207184 | tf_op jit(solution)/shard_map/all_gather | solution.py:193
  1020.3 32.1 %fusion.6 = bf16[528,768]{1,0:T(8,128)(2,1)S(1)} fusion(bf16[2088,768]{1,0:T(8,128)(2,1)} %convolution_convert_fusion.1), kind=kCustom, calls=%all-reduce-scatter.6 | all-reduce-scatter fusion | flops 1622017 | bytes 4018688
  1053.8 7.4 fusion.250
  1076.3 9.5 fusion.117
  1085.7 14.9 multiply_reduce_fusion.1
  1177.0 8.5 convert_reduce_fusion
  1186.6 9.0 add_convert_fusion.4
  1202.1 34.2 %fusion.7 = bf16[528,768]{1,0:T(8,128)(2,1)S(1)} fusion(bf16[2088,768]{1,0:T(8,128)(2,1)} %convolution_convert_fusion), kind=kCustom, calls=%all-reduce-scatter.7 | all-reduce-scatter fusion | flops 1622017 | bytes 4018688
  1237.7 9.4 add_convert_fusion.5
  1261.3 9.5 fusion.111
  1270.8 15.0 multiply_reduce_fusion
  1311.3 11.0 add_add_fusion
  1367.0 40.8 %all-reduce.9 = f32[18,768]{1,0:T(8,128)S(1)} all-reduce(f32[18,768]{1,0:T(8,128)S(1)} %pad_maximum_fusion.19), channel_id=11, replica_groups=mesh['items'=8,'ffn'=4] {'items','ffn'}, use_global_device_ids=true, to_apply=%region_85.86.clone | all-reduce | flops 13824 | bytes 110592
  1411.8 111.5 %reduce-scatter.24.cloned.1.call-done = f32[96,768]{1,0:T(8,128)} async-done(((f32[3072,768]{1,0:T(8,128)}), f32[96,768]{1,0:T(8,128)}) %reduce-scatter.24.cloned.1.call-update) | async-done | bytes 294928 | tf_op jit(solution)/shard_map/reduce_scatter | solution.py:269
  (815 shorter events, 524.1 us)
Async XLA Ops:
  7.2 70.2 %all-gather.20.cloned.1.call-start = ((), (), s32[]{:S(2)}) async-start(), calls=%async_computation.4 | async-start | bytes 4866048 | tf_op jit(solution)/shard_map/all_gather | solution.py:56
  7.9 131.2 %all-gather.26.cloned.1.call-start = ((), (), s32[]{:S(2)}) async-start(), calls=%async_computation.10 | async-start | bytes 4055040 | tf_op jit(solution)/shard_map/all_gather | solution.py:79
  53.6 53.1 %copy-start.133 = (f32[10,768]{1,0:T(8,128)}, f32[10,768]{1,0:T(8,128)S(1)}, u32[]{:S(2)}) copy-start(f32[10,768]{1,0:T(8,128)S(1)} %slice.306) | copy-start | bytes 92164
  65.9 40.8 %copy-start.58 = (f32[502,768]{1,0:T(8,128)}, f32[502,768]{1,0:T(8,128)S(1)}, u32[]{:S(2)}) copy-start(f32[502,768]{1,0:T(8,128)S(1)} %fusion.155) | copy-start | bytes 4626436
  109.4 163.4 %copy-start = (f32[522,768]{1,0:T(8,128)}, f32[522,768]{1,0:T(8,128)S(1)}, u32[]{:S(2)}) copy-start(f32[522,768]{1,0:T(8,128)S(1)} %get-tuple-element.155) | copy-start | bytes 4810756
  109.4 163.3 %copy-start.137 = (f32[522]{0:T(1024)}, f32[522]{0:T(1024)S(1)}, u32[]{:S(2)}) copy-start(f32[522]{0:T(1024)S(1)} %broadcast_multiply_fusion.23) | copy-start | bytes 6268
  109.7 163.0 %copy-start.143 = (f32[522]{0:T(1024)}, f32[522]{0:T(1024)S(1)}, u32[]{:S(2)}) copy-start(f32[522]{0:T(1024)S(1)} %add_rsqrt_fusion.7) | copy-start | bytes 6268
  111.0 71.3 %all-gather.22.cloned.1.call-start = ((), (), s32[]{:S(2)}) async-start(), calls=%async_computation.5 | async-start | bytes 1327104 | tf_op jit(solution)/shard_map/all_gather | solution.py:60
  111.7 112.5 %all-gather.24.cloned.1.call-start = ((), (), s32[]{:S(2)}) async-start(), calls=%async_computation.6 | async-start | bytes 1327104 | tf_op jit(solution)/shard_map/all_gather | solution.py:61
  112.3 225.5 %all-gather.28.cloned.1.call-start = ((), (), s32[]{:S(2)}) async-start(), calls=%async_computation.11 | async-start | bytes 4055040 | tf_op jit(solution)/shard_map/all_gather | solution.py:79
  230.8 34.9 %copy-start.60 = (bf16[1,1,502,768]{3,1,2,0:T(2,128)(2,1)S(1)}, bf16[1,1,502,768]{3,1,2,0:T(2,128)(2,1)}, u32[]{:S(2)}) copy-start(bf16[1,1,502,768]{3,1,2,0:T(2,128)(2,1)} %get-tuple-element.104) | copy-start | bytes 2313220
  264.5 3.8 collective-permute-start
  274.9 127.9 %copy-start.37 = (f32[1,522,768]{2,1,0:T(8,128)}, f32[1,522,768]{2,1,0:T(8,128)S(1)}, u32[]{:S(2)}) copy-start(f32[1,522,768]{2,1,0:T(8,128)S(1)} %add_bitcast_fusion.3) | copy-start | bytes 4810756
  277.0 27.1 %copy-start.157 = (f32[10,768]{1,0:T(8,128)}, f32[10,768]{1,0:T(8,128)S(1)}, u32[]{:S(2)}) copy-start(f32[10,768]{1,0:T(8,128)S(1)} %fusion.179) | copy-start | bytes 92164
  306.7 92.9 %copy-start.4 = (f32[522,768]{1,0:T(8,128)}, f32[522,768]{1,0:T(8,128)S(1)}, u32[]{:S(2)}) copy-start(f32[522,768]{1,0:T(8,128)S(1)} %get-tuple-element.161) | copy-start | bytes 4810756
  306.7 92.9 %copy-start.139 = (f32[522]{0:T(1024)}, f32[522]{0:T(1024)S(1)}, u32[]{:S(2)}) copy-start(f32[522]{0:T(1024)S(1)} %broadcast_multiply_fusion.21) | copy-start | bytes 6268
  307.1 92.5 %copy-start.147 = (f32[522]{0:T(1024)}, f32[522]{0:T(1024)S(1)}, u32[]{:S(2)}) copy-start(f32[522]{0:T(1024)S(1)} %add_rsqrt_fusion.5) | copy-start | bytes 6268
  308.4 155.4 %all-gather.30.cloned.1.call-start = ((), (), s32[]{:S(2)}) async-start(), calls=%async_computation.12 | async-start | bytes 4055040 | tf_op jit(solution)/shard_map/all_gather | solution.py:79
  388.6 5.0 collective-permute-start.1
  404.0 118.5 %copy-start.128 = (f32[1,10,768]{2,1,0:T(8,128)}, f32[1,10,768]{2,1,0:T(8,128)S(1)}, u32[]{:S(2)}) copy-start(f32[1,10,768]{2,1,0:T(8,128)S(1)} %slice_select_fusion.2) | copy-start | bytes 92164
  430.9 88.8 %copy-start.8 = (f32[522,768]{1,0:T(8,128)}, f32[522,768]{1,0:T(8,128)S(1)}, u32[]{:S(2)}) copy-start(f32[522,768]{1,0:T(8,128)S(1)} %get-tuple-element.167) | copy-start | bytes 4810756
  430.9 88.8 %copy-start.141 = (f32[522]{0:T(1024)}, f32[522]{0:T(1024)S(1)}, u32[]{:S(2)}) copy-start(f32[522]{0:T(1024)S(1)} %broadcast_multiply_fusion.19) | copy-start | bytes 6268
  431.3 88.5 %copy-start.151 = (f32[522]{0:T(1024)}, f32[522]{0:T(1024)S(1)}, u32[]{:S(2)}) copy-start(f32[522]{0:T(1024)S(1)} %add_rsqrt_fusion.3) | copy-start | bytes 6268
  432.5 35.6 %copy-start.204 = (bf16[768,768]{1,0:T(8,128)(2,1)S(1)}, bf16[768,768]{1,0:T(8,128)(2,1)}, u32[]{:S(2)}) copy-start(bf16[768,768]{1,0:T(8,128)(2,1)} %all-gather.22.cloned.1.call-done) | copy-start | bytes 3538948
  432.5 155.8 %all-gather.32.cloned.1.call-start = ((), (), s32[]{:S(2)}) async-start(), calls=%async_computation.13 | async-start | bytes 4055040 | tf_op jit(solution)/shard_map/all_gather | solution.py:79
  512.5 2.1 collective-permute-start.2
  523.7 26.9 %copy-start.159 = (f32[10,768]{1,0:T(8,128)}, f32[10,768]{1,0:T(8,128)S(1)}, u32[]{:S(2)}) copy-start(f32[10,768]{1,0:T(8,128)S(1)} %fusion.180) | copy-start | bytes 92164
  554.9 135.5 %all-gather.34.cloned.1.call-start = ((), (), s32[]{:S(2)}) async-start(), calls=%async_computation.14 | async-start | bytes 4055040 | tf_op jit(solution)/shard_map/all_gather | solution.py:193
  567.4 243.0 %copy-start.110 = (f32[1,10,768]{2,1,0:T(8,128)}, f32[1,10,768]{2,1,0:T(8,128)S(1)}, u32[]{:S(2)}) copy-start(f32[1,10,768]{2,1,0:T(8,128)S(1)} %broadcast.835) | copy-start | bytes 92164
  639.2 2.1 collective-permute-start.3
  656.9 189.7 %all-gather.36.cloned.1.call-start = ((), (), s32[]{:S(2)}) async-start(), calls=%async_computation.15 | async-start | bytes 4055040 | tf_op jit(solution)/shard_map/all_gather | solution.py:193
  708.3 35.3 %copy-start.171 = (f32[502]{0:T(512)S(1)}, f32[502]{0:T(512)}, u32[]{:S(2)}) copy-start(f32[502]{0:T(512)} %copy-done.170) | copy-start | bytes 6028
  742.0 5.0 collective-permute-start.4
  815.3 35.7 %copy-start.212 = (bf16[768,768]{0,1:T(8,128)(2,1)S(1)}, bf16[768,768]{0,1:T(8,128)(2,1)}, u32[]{:S(2)}) copy-start(bf16[768,768]{0,1:T(8,128)(2,1)} %all-gather.24.cloned.1.call-done) | copy-start | bytes 3538948
  815.4 187.5 %all-gather.38.cloned.1.call-start = ((), (), s32[]{:S(2)}) async-start(), calls=%async_computation.16 | async-start | bytes 4055040 | tf_op jit(solution)/shard_map/all_gather | solution.py:193
  864.7 35.1 %copy-start.20 = (bf16[1,1,502,768]{3,1,2,0:T(2,128)(2,1)S(1)}, bf16[1,1,502,768]{3,1,2,0:T(2,128)(2,1)}, u32[]{:S(2)}) copy-start(bf16[1,1,502,768]{3,1,2,0:T(2,128)(2,1)} %get-tuple-element.100) | copy-start | bytes 2313220
  864.7 35.1 %copy-start.177 = (f32[502]{0:T(512)S(1)}, f32[502]{0:T(512)}, u32[]{:S(2)}) copy-start(f32[502]{0:T(512)} %copy-done.176) | copy-start | bytes 6028
  898.4 3.5 collective-permute-start.5
  970.7 201.7 %all-gather.40.cloned.1.call-start = ((), (), s32[]{:S(2)}) async-start(), calls=%async_computation.17 | async-start | bytes 4055040 | tf_op jit(solution)/shard_map/all_gather | solution.py:193
  980.6 26.6 %copy-start.213 = (bf16[768,768]{0,1:T(8,128)(2,1)S(1)}, bf16[768,768]{0,1:T(8,128)(2,1)}, u32[]{:S(2)}) copy-start(bf16[768,768]{0,1:T(8,128)(2,1)} %all-gather.24.cloned.1.call-done) | copy-start | bytes 3538948
  1052.5 8.8 collective-permute-start.6
  1129.2 221.7 %reduce-scatter.30.cloned.1.call-start = ((), (), s32[]{:S(2)}) async-start(), calls=%async_computation.18 | async-start | bytes 221184
  1186.4 222.1 %reduce-scatter.28.cloned.1.call-start = ((), (), s32[]{:S(2)}) async-start(), calls=%async_computation.9 | async-start | bytes 1327104 | tf_op jit(solution)/shard_map/reduce_scatter | solution.py:276
  1195.7 214.4 %reduce-scatter.26.cloned.1.call-start = ((), (), s32[]{:S(2)}) async-start(), calls=%async_computation.8 | async-start | bytes 1327104 | tf_op jit(solution)/shard_map/reduce_scatter | solution.py:273
  1236.4 11.2 collective-permute-start.7
  1247.1 276.1 %reduce-scatter.24.cloned.1.call-start = ((), (), s32[]{:S(2)}) async-start(), calls=%async_computation.7 | async-start | bytes 9732096 | tf_op jit(solution)/shard_map/reduce_scatter | solution.py:269
  1261.3 24.5 %slice-start = ((s8[16220160]{0:T(1024)(128)(4,1)}), s8[4194304]{0:T(1024)(128)(4,1)S(1)}, s32[]{:S(2)}) async-start(s8[16220160]{0:T(1024)(128)(4,1)} %bitcast.428), calls=%async_computation.19 | async-start | bytes 8388608
  1261.3 24.5 %slice-start.1 = ((s8[16220160]{0:T(1024)(128)(4,1)}), s8[4194304]{0:T(1024)(128)(4,1)S(1)}, s32[]{:S(2)}) async-start(s8[16220160]{0:T(1024)(128)(4,1)} %bitcast.428), calls=%async_computation.20 | async-start | bytes 8388608
  (214 other events, 932.6 us)
Sparse Core Ops, SparseCore 0:
  10.9 66.3 all-gather.19
  111.1 27.8 all-gather.25
  141.3 41.0 all-gather.21
  184.4 39.8 all-gather.23
  308.5 29.2 all-gather.27
  432.6 31.0 all-gather.29
  555.0 33.2 all-gather.31
  657.1 33.2 all-gather.33
  815.5 31.0 all-gather.35
  970.8 31.9 all-gather.37
  1129.3 31.0 all-gather.39
  1186.5 63.0 reduce-scatter.29
  1253.0 63.0 reduce-scatter.27
  1319.3 62.9 reduce-scatter.25
  1388.6 134.5 reduce-scatter.23
where the time goes:
time: 1540 us; the launch traced here: 1530 us
  matrix products  419 us (27%)
  blocking collectives  368 us (24%)
  waiting for transfers between devices  362 us (24%)
  local copies, waits for them, and re-layouts  220 us (14%)
  other arithmetic  118 us (8%)
  starting transfers between devices  22.7 us (1%)
  between operations  20 us (1%)
    unnamed x10, blocking collectives  324 us
    unnamed x513, local copies, waits for them, and re-layouts  137 us
    reduce_scatter x1, waiting for transfers between devices, body(): lax.psum_scatter(attn_total, ('items', 'ffn'), scatter_dimension=0, tiled...  111 us
    all_gather x4, waiting for transfers between devices, body(): incoming = lax.all_gather(branch_low, 'ffn', axis=0, tiled=True)  86.8 us
    all_gather x4, waiting for transfers between devices, ffn_forward(): source = lax.all_gather(h_low, 'ffn', axis=0, tiled=True)  75.6 us
    dot_general x4, matrix products, body(): jnp.einsum('iqhd,ikhd->ihqk', grad_mixed, values, preferred_element_type=...  55.1 us
    all_gather x1, blocking collectives, body(): lax.all_gather(vectors, ('items', 'ffn'), axis=1, tiled=True)  44.1 us
    all_gather x1, waiting for transfers between devices, body(): lax.all_gather(w_in, 'items', axis=0, tiled=True)  38.8 us
  transfers between devices with their start and end apart: 23, of which 13 were waited for; matrix products, arithmetic and copies ran while one was open for 18% of the time, Pallas kernels for 0%

commit v1 on v0

v1 whole, which is shorter than its diff:
```python
import functools

import jax
import jax.numpy as jnp
from jax import lax
from jax.experimental import pallas as pl
from jax.experimental.pallas import tpu as pltpu
from jax.sharding import PartitionSpec as P

HEADS = 12
HD = 64
MEM = 10
TEXT = 502
SEGS_MAX = 4
ROWS = TEXT + MEM
AUG = 16

epsilon = 1e-12
root_half = 0.7071067811865476
inv_root_tau = 0.3989422804014327
log_two = 0.6931471805599453

f32 = jnp.float32
bf16 = jnp.bfloat16
AXES = ("items", "ffn")


def dot_nn(a, b):
    return jnp.dot(a, b, preferred_element_type=f32)


def dot_nt(a, b):
    return lax.dot_general(a, b, (((1,), (1,)), ((), ())), preferred_element_type=f32)


def dot_tn(a, b):
    return lax.dot_general(a, b, (((0,), (0,)), ((), ())), preferred_element_type=f32)


def split_three(value):
    high = value.astype(bf16)
    rest = value - high.astype(f32)
    mid = rest.astype(bf16)
    last = (rest - mid.astype(f32)).astype(bf16)
    return high, mid, last


def gelu_both(pre):
    half = 0.5 * (1.0 + lax.erf(pre * root_half))
    slope = half + pre * jnp.exp(-0.5 * pre * pre) * inv_root_tau
    return pre * half, slope


def norm_rows(value):
    centered = value - jnp.mean(value, axis=-1, keepdims=True)
    inverse = lax.rsqrt(jnp.mean(centered * centered, axis=-1, keepdims=True) + epsilon)
    return centered * inverse, inverse


def norm_rows_back(upstream, normed, inverse, gain):
    scaled = upstream * gain
    return inverse * (
        scaled
        - jnp.mean(scaled, axis=-1, keepdims=True)
        - normed * jnp.mean(scaled * normed, axis=-1, keepdims=True)
    )


def fill_limit(seg, count, fill):
    return jnp.where(seg < count, jnp.where(seg == count - 1, fill, TEXT), 0)


def aug_rows(first, second):
    width = first[0].shape[1]
    row = lax.broadcasted_iota(jnp.int32, (AUG, width), 0)
    out = jnp.zeros((AUG, width), f32)
    for place, piece in enumerate(tuple(first) + tuple(second)):
        out = jnp.where(row == place, jnp.broadcast_to(piece.astype(f32), (AUG, width)), out)
    return out.astype(bf16)


def ones_three(width):
    one = jnp.ones((1, width), bf16)
    return (one, one, one)


def key_bias(limit):
    place = lax.broadcasted_iota(jnp.int32, (1, ROWS), 1)
    bias = jnp.where(place < limit, 0.0, jnp.where(place < TEXT, -1e9, log_two)).astype(f32)
    return split_three(bias)


def forward_kernel(
    count_ref, fill_ref, text_ref, attn_ref, win_ref, wout_ref, bin_ref, vec_ref, col_ref,
    out_ref, mem_ref, zl_ref, qkv_ref, mixed_ref, lse_ref, n1_ref, r1_ref, hl_ref, act_ref,
    slope_ref, n2_ref, r2_ref,
    memory, z_ref, h_ref, acc_ref,
):
    seg = pl.program_id(0)
    count, fill = count_ref[0], fill_ref[0]
    limit = fill_limit(seg, count, fill)
    width = z_ref.shape[1]

    @pl.when(seg == 0)
    def _():
        memory[...] = vec_ref[8 : 8 + MEM, :]

    z_ref[:TEXT, :] = text_ref[0].astype(f32)
    z_ref[TEXT:, :] = memory[...]
    zl = z_ref[...].astype(bf16)
    zl_ref[...] = zl
    for c in range(3):
        part = dot_nt(attn_ref[c * width : (c + 1) * width, :], zl)
        if c == 0:
            part = (part + col_ref[:, 0:1]).astype(bf16) * jnp.asarray(HD ** (-0.5), bf16)
        elif c == 2:
            part = (part + col_ref[:, 1:2]).astype(bf16)
        else:
            part = part.astype(bf16)
        qkv_ref[c * width : (c + 1) * width, :] = part

    ones = ones_three(ROWS)
    key_aug = aug_rows(key_bias(limit), ())
    query_aug = aug_rows(ones, ())
    for head in range(HEADS):
        lo = head * HD
        q_aug = jnp.concatenate([qkv_ref[lo : lo + HD, :], query_aug], axis=0)
        k_aug = jnp.concatenate([qkv_ref[width + lo : width + lo + HD, :], key_aug], axis=0)
        v_aug = jnp.concatenate([qkv_ref[2 * width + lo : 2 * width + lo + HD, :], query_aug], axis=0)
        scores = dot_tn(k_aug, q_aug)
        peak = jnp.max(scores, axis=0, keepdims=True)
        expo = jnp.exp(scores - peak).astype(bf16)
        both = dot_nn(v_aug, expo)
        total = both[HD : HD + 1, :]
        mixed_ref[lo : lo + HD, :] = (both[:HD, :] * (1.0 / total)).astype(bf16)
        lse_ref[0, head : head + 1, :] = peak + jnp.log(total)

    first = z_ref[...] + (dot_tn(mixed_ref[...], attn_ref[3 * width :, :]) + vec_ref[2:3, :])
    normed, inverse = norm_rows(first)
    n1_ref[...] = normed.astype(bf16)
    r1_ref[...] = inverse
    h = normed * vec_ref[3:4, :] + vec_ref[4:5, :]
    h_ref[...] = h
    hl_ref[...] = h.astype(bf16)

    blocks, _, block = win_ref.shape
    for f in range(blocks):
        pre = dot_nn(hl_ref[...], win_ref[f]) + bin_ref[f : f + 1, :]
        act, slope = gelu_both(pre)
        act_ref[:, f * block : (f + 1) * block] = act.astype(bf16)
        slope_ref[:, f * block : (f + 1) * block] = slope.astype(bf16)
        part = dot_nt(act_ref[:, f * block : (f + 1) * block], wout_ref[f])
        if f == 0:
            acc_ref[...] = part
        else:
            acc_ref[...] += part

    normed, inverse = norm_rows(h_ref[...] + (acc_ref[...] + vec_ref[5:6, :]))
    n2_ref[...] = normed.astype(bf16)
    r2_ref[...] = inverse
    y = normed * vec_ref[6:7, :] + vec_ref[7:8, :]
    row = lax.broadcasted_iota(jnp.int32, (TEXT, 1), 0)
    out_ref[0] = jnp.where(row < limit, y[:TEXT, :], 0.0).astype(bf16)
    memory[...] = jnp.where(seg < count, y[TEXT:, :], memory[...])
    mem_ref[...] = memory[...]


def backward_kernel(
    count_ref, fill_ref, grad_ref, mgrad_ref, attn_ref, win_ref, wout_ref, vec_ref,
    qkv_ref, mixed_ref, lse_ref, n1_ref, r1_ref, slope_ref, n2_ref, r2_ref,
    tgrad_ref, gbranch_ref, gpre_ref, gattn_ref, gqkv_ref, vgrad_ref, bgrad_ref, gmem_ref,
    gm_ref, gy_ref, second_ref, acc_ref, mix_ref, cols_ref,
):
    step = pl.program_id(0)
    seg = SEGS_MAX - 1 - step
    count, fill = count_ref[0], fill_ref[0]
    limit = fill_limit(seg, count, fill)
    width = gy_ref.shape[1]

    @pl.when(step == 0)
    def _():
        gm_ref[...] = mgrad_ref[0]
        vgrad_ref[...] = jnp.zeros_like(vgrad_ref)
        bgrad_ref[...] = jnp.zeros_like(bgrad_ref)

    row = lax.broadcasted_iota(jnp.int32, (TEXT, 1), 0)
    gy_ref[:TEXT, :] = jnp.where(row < limit, grad_ref[0].astype(f32), 0.0)
    gy_ref[TEXT:, :] = jnp.where(seg < count, gm_ref[...], 0.0)

    def column_sum(value):
        return jnp.sum(value, axis=0, keepdims=True)

    gy = gy_ref[...]
    normed = n2_ref[...].astype(f32)
    vgrad_ref[6:7, :] += column_sum(gy * normed)
    vgrad_ref[7:8, :] += column_sum(gy)
    second = norm_rows_back(gy, normed, r2_ref[...], vec_ref[6:7, :])
    second_ref[...] = second
    gbranch_ref[...] = second.astype(bf16)
    vgrad_ref[5:6, :] += column_sum(gbranch_ref[...].astype(f32))

    blocks, _, block = win_ref.shape
    for f in range(blocks):
        sl = slice(f * block, (f + 1) * block)
        hidden = dot_nn(gbranch_ref[...], wout_ref[f])
        pre = (hidden * slope_ref[:, sl].astype(f32)).astype(bf16)
        gpre_ref[:, sl] = pre
        bgrad_ref[f : f + 1, :] += column_sum(pre.astype(f32))
        part = dot_nt(gpre_ref[:, sl], win_ref[f])
        if f == 0:
            acc_ref[...] = part
        else:
            acc_ref[...] += part

    gh = second_ref[...] + acc_ref[...]
    normed = n1_ref[...].astype(f32)
    vgrad_ref[3:4, :] += column_sum(gh * normed)
    vgrad_ref[4:5, :] += column_sum(gh)
    first = norm_rows_back(gh, normed, r1_ref[...], vec_ref[3:4, :])
    second_ref[...] = first
    gattn_ref[...] = first.astype(bf16)
    vgrad_ref[2:3, :] += column_sum(gattn_ref[...].astype(f32))
    mix_ref[...] = dot_nt(attn_ref[3 * width :, :], gattn_ref[...]).astype(bf16)

    ones = ones_three(ROWS)
    key_aug = aug_rows(key_bias(limit), ones)
    value_aug = aug_rows(ones, ())
    for head in range(HEADS):
        lo = head * HD
        q_h = qkv_ref[lo : lo + HD, :]
        k_h = qkv_ref[width + lo : width + lo + HD, :]
        v_h = qkv_ref[2 * width + lo : 2 * width + lo + HD, :]
        g_h = mix_ref[lo : lo + HD, :]
        inner = column_sum(g_h.astype(f32) * mixed_ref[lo : lo + HD, :].astype(f32))
        q_aug = jnp.concatenate([q_h, aug_rows(ones, split_three(-lse_ref[0, head : head + 1, :]))], axis=0)
        k_aug = jnp.concatenate([k_h, key_aug], axis=0)
        v_aug = jnp.concatenate([v_h, value_aug], axis=0)
        g_aug = jnp.concatenate([g_h, aug_rows(split_three(-inner), ())], axis=0)
        probs = jnp.exp(dot_tn(k_aug, q_aug))
        grads = (probs * dot_tn(v_aug, g_aug)).astype(bf16)
        probs_low = probs.astype(bf16)
        cols_ref[lo : lo + HD, :] = dot_nn(k_h, grads) * (HD ** (-0.5))
        cols_ref[width + lo : width + lo + HD, :] = dot_nt(q_h, grads)
        cols_ref[2 * width + lo : 2 * width + lo + HD, :] = dot_nt(g_h, probs_low)

    for c in range(3):
        gqkv_ref[:, c * width : (c + 1) * width] = cols_ref[c * width : (c + 1) * width, :].T.astype(bf16)
    vgrad_ref[0:1, :] += column_sum(gqkv_ref[:, :width].astype(f32))
    vgrad_ref[1:2, :] += column_sum(gqkv_ref[:, 2 * width :].astype(f32))
    joined = second_ref[...]
    for c in range(3):
        joined = joined + dot_nt(gqkv_ref[:, c * width : (c + 1) * width], attn_ref[c * width : (c + 1) * width, :])
    acc_ref[...] = joined
    tgrad_ref[0] = acc_ref[:TEXT, :]
    gm_ref[...] = jnp.where(seg < count, acc_ref[TEXT:, :], gm_ref[...])
    gmem_ref[...] = gm_ref[...]


def whole():
    return pl.BlockSpec(memory_space=pltpu.VMEM)


def scalar():
    return pl.BlockSpec(memory_space=pltpu.SMEM)


def forward_call(count, fill, text, attn_t, win, wout, bias, vec, col):
    width = text.shape[-1]
    hidden = win.shape[0] * win.shape[2]
    total = SEGS_MAX * ROWS

    def rows(cols):
        return pl.BlockSpec((ROWS, cols), lambda s: (s, 0))

    def lanes(height):
        return pl.BlockSpec((height, ROWS), lambda s: (0, s))

    seg_block = pl.BlockSpec((1, TEXT, width), lambda s: (s, 0, 0))
    sds = jax.ShapeDtypeStruct
    return pl.pallas_call(
        forward_kernel,
        grid=(SEGS_MAX,),
        in_specs=[scalar(), scalar(), seg_block] + [whole()] * 6,
        out_specs=[
            seg_block, pl.BlockSpec((MEM, width), lambda s: (0, 0)),
            rows(width), lanes(3 * width), lanes(width),
            pl.BlockSpec((1, 16, ROWS), lambda s: (s, 0, 0)),
            rows(width), rows(1), rows(width), rows(hidden), rows(hidden), rows(width), rows(1),
        ],
        out_shape=[
            sds((SEGS_MAX, TEXT, width), bf16), sds((MEM, width), f32),
            sds((total, width), bf16), sds((3 * width, total), bf16), sds((width, total), bf16),
            sds((SEGS_MAX, 16, ROWS), f32),
            sds((total, width), bf16), sds((total, 1), f32), sds((total, width), bf16),
            sds((total, hidden), bf16), sds((total, hidden), bf16), sds((total, width), bf16),
            sds((total, 1), f32),
        ],
        scratch_shapes=[
            pltpu.VMEM((MEM, width), f32), pltpu.VMEM((ROWS, width), f32),
            pltpu.VMEM((ROWS, width), f32), pltpu.VMEM((ROWS, width), f32),
        ],
        compiler_params=pltpu.CompilerParams(vmem_limit_bytes=62 * 2**20),
    )(count, fill, text, attn_t, win, wout, bias, vec, col)


def backward_call(count, fill, out_grad, mem_grad, attn, win, wout, vec, saved):
    width = out_grad.shape[-1]
    blocks, _, block = win.shape
    hidden = blocks * block
    total = SEGS_MAX * ROWS
    last = SEGS_MAX - 1

    def rows(cols):
        return pl.BlockSpec((ROWS, cols), lambda s: (last - s, 0))

    def lanes(height):
        return pl.BlockSpec((height, ROWS), lambda s: (0, last - s))

    def fixed(*shape):
        return pl.BlockSpec(shape, lambda s: (0,) * len(shape))

    seg_block = pl.BlockSpec((1, TEXT, width), lambda s: (last - s, 0, 0))
    sds = jax.ShapeDtypeStruct
    return pl.pallas_call(
        backward_kernel,
        grid=(SEGS_MAX,),
        in_specs=[scalar(), scalar(), seg_block] + [whole()] * 5
        + [
            lanes(3 * width), lanes(width), pl.BlockSpec((1, 16, ROWS), lambda s: (last - s, 0, 0)),
            rows(width), rows(1), rows(hidden), rows(width), rows(1),
        ],
        out_specs=[
            seg_block, rows(width), rows(hidden), rows(width), rows(3 * width),
            fixed(8, width), fixed(blocks, block), fixed(MEM, width),
        ],
        out_shape=[
            sds((SEGS_MAX, TEXT, width), f32), sds((total, width), bf16), sds((total, hidden), bf16),
            sds((total, width), bf16), sds((total, 3 * width), bf16),
            sds((8, width), f32), sds((blocks, block), f32), sds((MEM, width), f32),
        ],
        scratch_shapes=[
            pltpu.VMEM((MEM, width), f32), pltpu.VMEM((ROWS, width), f32),
            pltpu.VMEM((ROWS, width), f32), pltpu.VMEM((ROWS, width), f32),
            pltpu.VMEM((width, ROWS), bf16), pltpu.VMEM((3 * width, ROWS), f32),
        ],
        compiler_params=pltpu.CompilerParams(vmem_limit_bytes=62 * 2**20),
    )(count, fill, out_grad, mem_grad, attn, win, wout, vec, *saved)


def body(n_items, n_ffn, text_rows, attn_weight, vectors, w_in, b_in, w_out, seg_count, last_fill, out_grad, mem_grad):
    width = text_rows.shape[-1]
    block = w_in.shape[1]
    attn = lax.all_gather(attn_weight, AXES, axis=0, tiled=True)
    vec = lax.all_gather(vectors, AXES, axis=1, tiled=True).astype(f32)

    def by_block(shard):
        parts = lax.all_gather(shard, AXES, axis=0).reshape(n_items, n_ffn, width // n_items, block)
        return parts.transpose(1, 0, 2, 3).reshape(n_ffn, width, block)

    win = by_block(w_in)
    wout = by_block(w_out.T)
    bias = lax.all_gather(b_in, AXES, axis=0).reshape(n_items, n_ffn, -1)
    bias = bias.transpose(1, 0, 2).reshape(n_ffn, block).astype(f32)
    attn_t = jnp.concatenate(
        [attn[: 3 * width].reshape(3, width, width).transpose(0, 2, 1).reshape(3 * width, width), attn[3 * width :]]
    )
    col = vec[:2].T

    (activations, memory, zl, qkv, mixed, lse, n1, r1, hl, act, slope, n2, r2) = forward_call(
        seg_count, last_fill, text_rows[0], attn_t, win, wout, bias, vec, col
    )
    text_grad, gbranch, gpre, gattn, gqkv, vgrad, bgrad, gmem = backward_call(
        seg_count, last_fill, out_grad[0], mem_grad, attn, win, wout, vec,
        (qkv, mixed, lse, n1, r1, slope, n2, r2),
    )

    def scatter_block(grad):
        grad = grad.astype(bf16).reshape(n_items, width // n_items, n_ffn, block).transpose(0, 2, 1, 3)
        return lax.psum_scatter(grad.reshape(n_items * n_ffn, width // n_items, block), AXES, scatter_dimension=0, tiled=False).astype(f32)

    w_out_grad = scatter_block(dot_tn(gbranch, act)).T
    w_in_grad = scatter_block(dot_tn(hl, gpre))
    three = dot_tn(zl, gqkv)
    attn_total = jnp.concatenate(
        [three[:, c * width : (c + 1) * width] for c in range(3)] + [dot_nn(mixed, gattn)], axis=0
    ).astype(bf16)
    attn_grad = lax.psum_scatter(attn_total, AXES, scatter_dimension=0, tiled=True).astype(f32)
    vec_total = jnp.concatenate([vgrad, gmem], axis=0)
    vector_grad = lax.psum_scatter(vec_total, AXES, scatter_dimension=1, tiled=True)
    b_total = bgrad.reshape(n_ffn, n_items, block // n_items).transpose(1, 0, 2).reshape(n_items * n_ffn, 1, block // n_items)
    b_in_grad = lax.psum_scatter(b_total, AXES, scatter_dimension=0, tiled=False)
    return (activations[None], memory[None], text_grad[None], attn_grad, vector_grad, w_in_grad, b_in_grad, w_out_grad)


def solution(mesh):
    both = P(AXES)
    return jax.shard_map(
        functools.partial(body, mesh.shape["items"], mesh.shape["ffn"]),
        mesh=mesh,
        in_specs=(
            both, both, P(None, AXES), P("items", "ffn"), P("ffn", "items"), P("ffn", "items"),
            both, both, both, both,
        ),
        out_specs=(both, both, both, both, P(None, AXES), P("items", "ffn"), P("ffn", "items"), P("ffn", "items")),
        check_vma=False,
    )
```

time: 1540 us -> 861 us (0.56)
  matrix products: 419 us -> 44.1 us
  blocking collectives: 368 us -> 80.8 us
  Pallas kernels: 0 us -> 157 us
  local copies, waits for them, and re-layouts: 220 us -> 75.9 us
  waiting for transfers between devices: 362 us -> 471 us
  other arithmetic: 118 us -> 12.6 us
  starting transfers between devices: 22.7 us -> 0.28 us
    dot_general x68 -> x4, matrix products: 382 us -> 44.1 us  [the longest x3 37.5 us: dot_tn(): lax.dot_general(a, b, (((0,), (0,)), ((), ())), preferred_element_type=f32)]
    unnamed x10 -> x0, blocking collectives: 324 us -> none
    reduce_scatter x3, waiting for transfers between devices: 111 us -> 332 us  [the longest x2 221 us: scatter_block(): lax.psum_scatter(grad.reshape(n_items * n_ffn, width // n_items, block),...]
    pallas_call x0 -> x2, Pallas kernels: none -> 157 us  [the longest x1 86.9 us: backward_call(): pl.pallas_call(backward_kernel, grid=(SEGS_MAX,), in_specs=[scalar(), sca...]
    all_gather x11 -> x3, waiting for transfers between devices: 247 us -> 97.4 us  [the longest x2 97.4 us: by_block(): lax.all_gather(shard, AXES, axis=0)]
    unnamed x513 -> x32, local copies, waits for them, and re-layouts: 137 us -> 25.4 us
    slice x26 -> x5, local copies, waits for them, and re-layouts: 50.5 us -> 2.23 us  [the longest x2 2 us: body(): attn[:3 * width].reshape(3, width, width).transpose(0, 2, 1)]
    reduce_sum x47 -> x0, other arithmetic: 47.7 us -> none  [the longest x8 16.3 us: norm_backward(): jnp.sum(upstream * normed, axis=(0, 1))]
  transfers between devices with their start and end apart: 23 -> 7, of which waited for: 13 -> 6; matrix products, arithmetic and copies ran while one was open for 18% -> 11% of each run, Pallas kernels for 0% -> 0%
where the time goes in v1:
time: 861 us; the launch traced here: 857 us
  waiting for transfers between devices  471 us (55%)
  Pallas kernels  157 us (18%)
  blocking collectives  80.8 us (9%)
  local copies, waits for them, and re-layouts  75.9 us (9%)
  matrix products  44.1 us (5%)
  between operations  15.8 us (2%)
  other arithmetic  12.6 us (1%)
    reduce_scatter x2, waiting for transfers between devices, scatter_block(): lax.psum_scatter(grad.reshape(n_items * n_ffn, width // n_items, block),...  221 us
    reduce_scatter x1, waiting for transfers between devices, body(): lax.psum_scatter(attn_total, AXES, scatter_dimension=0, tiled=True)  111 us
    all_gather x2, waiting for transfers between devices, by_block(): lax.all_gather(shard, AXES, axis=0)  97.4 us
    pallas_call x1, Pallas kernels, backward_call(): pl.pallas_call(backward_kernel, grid=(SEGS_MAX,), in_specs=[scalar(), sca...  86.9 us
    pallas_call x1, Pallas kernels, forward_call(): pl.pallas_call(forward_kernel, grid=(SEGS_MAX,), in_specs=[scalar(), scal...  69.9 us
    all_gather x1, blocking collectives, body(): bias = lax.all_gather(b_in, AXES, axis=0).reshape(n_items, n_ffn, -1)  43.2 us
    unnamed x8, waiting for transfers between devices  41.4 us
    all_gather x1, blocking collectives, body(): vec = lax.all_gather(vectors, AXES, axis=1, tiled=True).astype(f32)  37.6 us
  transfers between devices with their start and end apart: 7, of which 6 were waited for; matrix products, arithmetic and copies ran while one was open for 11% of the time, Pallas kernels for 0%

profile of v1, /device:TPU:0, one launch (start us, length us, event | category | flops | bytes accessed | tf_op | source)
XLA Modules:
  0.0 856.9 jit_solution(5047359624004614663)
XLA Ops:
  7.2 0.7 all-gather.8.cloned.1.call-update
  8.0 0.7 all-gather.10.cloned.1.call-update
  8.7 0.7 all-gather.12.cloned.1.call-update
  10.8 3.9 copy.54
  14.6 43.2 %all-gather.3 = bf16[32,1,96]{2,1,0:T(2,128)(2,1)S(1)} all-gather(bf16[1,1,96]{2,1,0:T(2,128)(2,1)S(1)} %bitcast.77), channel_id=4, replica_groups=mesh['items'=8,'ffn'=4] {'items','ffn'}, dimensions={0}, use_global_device_ids=true | all-gather | bytes 6336 | tf_op jit(solution)/shard_map/all_gather | solution.py:362
  57.8 0.7 reshape.74.bin_ref
  58.6 37.6 %all_gather.31 = bf16[18,768]{0,1:T(8,128)(2,1)S(1)} all-gather(bf16[18,24]{0,1:T(8,128)(2,1)S(1)} %copy.37), channel_id=1, replica_groups=mesh['items'=8,'ffn'=4] {'items','ffn'}, dimensions={1}, use_global_device_ids=true | all-gather | bytes 28512 | tf_op jit(solution)/shard_map/all_gather | solution.py:354
  96.3 0.6 copy-done.3
  97.0 1.0 copy.39.col_ref
  98.0 2.0 copy.53
  100.0 0.6 copy.41.mgrad_ref
  100.6 2.0 slice-done
  102.6 3.7 copy.33
  106.3 37.0 %all-gather.10.cloned.1.call-done = bf16[3072,768]{1,0:T(8,128)(2,1)} async-done(((bf16[96,768]{1,0:T(8,128)(2,1)}), bf16[3072,768]{1,0:T(8,128)(2,1)}) %all-gather.10.cloned.1.call-update) | async-done | bytes 4718608 | tf_op jit(solution)/shard_map/all_gather | solution.py:357
  143.2 4.9 copy.34
  148.1 60.4 %all-gather.12.cloned.1.call-done = bf16[3072,768]{1,0:T(8,128)(2,1)} async-done(((bf16[96,768]{1,0:T(8,128)(2,1)}), bf16[3072,768]{1,0:T(8,128)(2,1)}) %all-gather.12.cloned.1.call-update) | async-done | bytes 4718608 | tf_op jit(solution)/shard_map/all_gather | solution.py:357
  208.6 5.0 copy.35
  213.6 2.5 pad_maximum_fusion.attn_ref
  216.1 69.9 %shard_map.161 = (bf16[4,502,768]{2,1,0:T(8,128)(2,1)}, f32[10,768]{1,0:T(8,128)}, bf16[2048,768]{1,0:T(8,128)(2,1)}, bf16[2304,2048]{1,0:T(8,128)(2,1)}, bf16[7...) custom-call(s32[1]{0:T(128)S(6)} %copy.58.count_ref, ...), custom_call_target="tpu_custom_call" | custom-call | tf_op jit(solution)/shard_map/pallas_call | solution.py:280
  286.0 86.9 %shard_map.162 = (f32[4,502,768]{2,1,0:T(8,128)}, bf16[2048,768]{1,0:T(8,128)(2,1)}, bf16[2048,3072]{1,0:T(8,128)(2,1)}, bf16[2048,768]{1,0:T(8,128)(2,1)}, bf16...) custom-call(s32[1]{0:T(128)S(6)} %copy.58.count_ref, s32[1]{0:T(128)S(6)} %copy.59.fill_ref, ...), custom_call_target="tpu_custom_call" | custom-call | tf_op jit(solution)/shard_map/pallas_call | solution.py:324
  372.9 6.6 convolution_convert_fusion.3
  379.5 8.5 convolution_convert_fusion.2
  388.0 0.2 fusion.1
  388.2 0.8 reshape.70
  389.0 0.6 copy.43
  389.6 1.4 pad_maximum_fusion.2
  391.1 3.7 pad_maximum_fusion.1
  395.0 1.8 copy-done.10
  396.8 14.4 %convolution_convert_fusion.1 = bf16[768,3072]{1,0:T(8,128)(2,1)} fusion(bf16[2048,768]{1,0:T(8,128)(2,1)S(1)} %copy-done.10, bf16[2048,3072]{1,0:T(8,128)(2,1)} %get-tuple-element.46), kind=kOutput, calls=%fused_computation.1 | convolution fusion | flops 9666035712 | bytes 20447232 | tf_op jit(solution)/shard_map/dot_general | solution.py:37
  411.2 9.8 %reshape.68 = bf16[8,96,4,768]{3,2,1,0:T(4,128)(2,1)} reshape(bf16[768,3072]{1,0:T(8,128)(2,1)} %convolution_convert_fusion.1) | data formatting | bytes 9437184 | tf_op jit(solution)/shard_map/reshape | solution.py:378
  420.9 5.4 copy.42
  426.4 1.8 copy-done.9
  428.2 14.6 %convolution_convert_fusion = bf16[768,3072]{1,0:T(8,128)(2,1)} fusion(bf16[2048,768]{1,0:T(8,128)(2,1)S(1)} %copy-done.9, bf16[2048,3072]{1,0:T(8,128)(2,1)} %get-tuple-element.49), kind=kOutput, calls=%fused_computation | convolution fusion | flops 9666035712 | bytes 20447232 | tf_op jit(solution)/shard_map/dot_general | solution.py:37
  442.8 9.7 %reshape.72 = bf16[8,96,4,768]{3,2,1,0:T(4,128)(2,1)} reshape(bf16[768,3072]{1,0:T(8,128)(2,1)} %convolution_convert_fusion) | data formatting | bytes 9437184 | tf_op jit(solution)/shard_map/reshape | solution.py:378
  452.6 5.4 copy.44
  458.0 1.9 copy-done.1
  459.9 2.8 copy.45
  462.7 0.6 copy.46
  463.3 7.8 copy.47
  471.1 39.2 %all-reduce.5.cloned.1.call-done = (f32[18,768]{1,0:T(8,128)}, f32[32,1,96]{2,1,0:T(1,128)}) async-done(((f32[18,768]{1,0:T(8,128)}, f32[32,1,96]{2,1,0:T(1,128)}), (f32[18,768]{1,0:T(8,128)}, f32[32,1,96]{2,1,0:T(1,128)})) %all-reduce.5.cloned.1.call-update) | async-done | bytes 67600
  510.4 1.1 fusion
  511.5 1.4 constant_dynamic-slice_fusion.1
  512.9 111.3 %reduce-scatter.5.cloned.1.call-done = bf16[96,768]{1,0:T(8,128)(2,1)} async-done(((bf16[3072,768]{1,0:T(8,128)(2,1)}), bf16[96,768]{1,0:T(8,128)(2,1)}) %reduce-scatter.5.cloned.1.call-update) | async-done | bytes 147472 | tf_op jit(solution)/shard_map/reduce_scatter | solution.py:387
  624.2 1.6 convert_element_type.37
  625.9 110.7 %reduce-scatter.7.cloned.1.call-done = bf16[1,96,768]{2,1,0:T(8,128)(2,1)} async-done(((bf16[32,96,768]{2,1,0:T(8,128)(2,1)}), bf16[1,96,768]{2,1,0:T(8,128)(2,1)}) %reduce-scatter.7.cloned.1.call-update) | async-done | bytes 147472 | tf_op jit(solution)/shard_map/reduce_scatter | solution.py:379
  736.6 1.6 bitcast_convert_fusion
  738.2 109.9 %reduce-scatter.9.cloned.1.call-done = bf16[1,96,768]{2,1,0:T(8,128)(2,1)} async-done(((bf16[32,96,768]{2,1,0:T(8,128)(2,1)}), bf16[1,96,768]{2,1,0:T(8,128)(2,1)}) %reduce-scatter.9.cloned.1.call-update) | async-done | bytes 147472 | tf_op jit(solution)/shard_map/reduce_scatter | solution.py:379
  848.1 1.6 convert_bitcast_fusion
  (41 shorter events, 0.6 us)
Async XLA Ops:
  7.2 7.4 copy-start.7
  7.2 51.3 %copy-start.6 = (bf16[18,24]{1,0:T(8,128)(2,1)S(1)}, bf16[18,24]{1,0:T(8,128)(2,1)}, u32[]{:S(2)}) copy-start(bf16[18,24]{1,0:T(8,128)(2,1)} %param.12) | copy-start | bytes 2596
  7.2 90.8 %copy-start.2 = (bf16[1,4,502,768]{3,1,2,0:T(4,128)(2,1)S(1)}, bf16[1,4,502,768]{3,1,2,0:T(4,128)(2,1)}, u32[]{:S(2)}) copy-start(bf16[1,4,502,768]{3,1,2,0:T(4,128)(2,1)} %param.18) | copy-start | bytes 9252868
  7.2 93.4 %all-gather.8.cloned.1.call-start = ((), (), s32[]{:S(2)}) async-start(), calls=%async_computation.3 | async-start | bytes 4866048 | tf_op jit(solution)/shard_map/all_gather | solution.py:353
  7.9 135.3 %all-gather.10.cloned.1.call-start = ((), (), s32[]{:S(2)}) async-start(), calls=%async_computation.7 | async-start | bytes 4866048 | tf_op jit(solution)/shard_map/all_gather | solution.py:357
  8.7 199.9 %all-gather.12.cloned.1.call-start = ((), (), s32[]{:S(2)}) async-start(), calls=%async_computation.8 | async-start | bytes 4866048 | tf_op jit(solution)/shard_map/all_gather | solution.py:357
  9.4 501.0 %all-reduce.5.cloned.1.call-start = ((), (), s32[]{:S(2)}) async-start(), calls=%async_computation.9 | async-start | bytes 180224
  14.6 85.4 %copy-start.5 = (f32[1,10,768]{2,0,1:T(1,128)S(1)}, f32[1,10,768]{2,0,1:T(1,128)}, u32[]{:S(2)}) copy-start(f32[1,10,768]{2,0,1:T(1,128)} %param.19) | copy-start | bytes 92164
  96.3 0.6 copy-start.3
  100.6 2.0 slice-start
  208.6 5.0 slice-start.1
  208.6 5.0 copy-start
  372.8 6.6 copy-start.8
  372.8 6.6 copy-start.11
  391.1 233.2 %reduce-scatter.5.cloned.1.call-start = ((), (), s32[]{:S(2)}) async-start(), calls=%async_computation.4 | async-start | bytes 4866048 | tf_op jit(solution)/shard_map/reduce_scatter | solution.py:387
  394.9 1.9 copy-start.10
  394.9 341.7 %reduce-scatter.7.cloned.1.call-start = ((), (), s32[]{:S(2)}) async-start(), calls=%async_computation.5 | async-start | bytes 4866048 | tf_op jit(solution)/shard_map/reduce_scatter | solution.py:379
  426.3 1.9 copy-start.9
  426.4 421.8 %reduce-scatter.9.cloned.1.call-start = ((), (), s32[]{:S(2)}) async-start(), calls=%async_computation.6 | async-start | bytes 4866048 | tf_op jit(solution)/shard_map/reduce_scatter | solution.py:379
  458.0 1.9 copy-start.1
  458.0 4.7 copy-start.4
Sparse Core Ops, SparseCore 0:
  10.9 66.9 all-gather.7
  80.9 62.3 all-gather.9
  146.1 62.3 all-gather.11
  391.2 119.1 all-reduce.4
  515.7 108.4 reduce-scatter.4
  630.5 106.0 reduce-scatter.6
  742.0 106.0 reduce-scatter.8
